TPU v7x, 32 devices: a whole 2x2x4 slice. The times are simulated.
32 devices in a mesh: groups: 2 (over x), wide: 16 (over z, y, core).
Axes of the slice: x: 2, y: 2, z: 4, core: 2. Of those that a mesh axis runs over, the one named last changes fastest.
Arguments:
- gate_pre: bfloat16 [1024, 32768], P('groups', 'wide'), parts along dimension 0, may hold values from -8 to 8
- up_pre: bfloat16 [1024, 32768], P('groups', 'wide'), parts along dimension 0, may hold values from -8 to 8
- down_weight: bfloat16 [32768, 8192], P('wide'), may hold values from -0.03125 to 0.03125
Outputs:
- block_out: bfloat16 [1024, 8192], P(('groups', 'wide')), parts along dimension 0
There are 2 independent parts, one for each index of `groups`. A program takes and returns all parts, laid end to end along the dimension named above; an argument that names none is the same for every part. Nothing has to cross between parts.
All inputs are finite; a program needn't handle non-finite values.
Results may differ from a plain program's by a relative error of at most 0.005.
Values may be sent and summed in bfloat16 or wider, within the bound.
A program may use at most 128 MiB of HBM per device.

v0:
```python
import jax
import jax.numpy as jnp
from jax import lax
from jax.sharding import PartitionSpec as P


def per_device(gate_pre, up_pre, down_weight):
    hidden = (jax.nn.silu(gate_pre.astype(jnp.float32)) * up_pre.astype(jnp.float32)).astype(
        jnp.bfloat16
    )
    summed = lax.psum_scatter(
        jnp.dot(hidden, down_weight, preferred_element_type=jnp.float32),
        "wide",
        scatter_dimension=0,
        tiled=True,
    )
    return summed.astype(jnp.bfloat16)


def solution(mesh):
    in_specs = (P("groups", "wide"), P("groups", "wide"), P("wide", None))
    out_specs = P(("groups", "wide"), None)
    return jax.shard_map(
        per_device, mesh=mesh, in_specs=in_specs, out_specs=out_specs, check_vma=False
    )
```

profile of v0, /device:TPU:0, one launch (start us, length us, event | category | flops | bytes accessed | tf_op | source)
XLA Modules:
  0.0 225.4 jit_solution(4750876946602921799)
XLA Ops:
  6.5 0.0 reduce-scatter.2.cloned.1.call-start
  6.5 28.5 %fusion.5 = f32[512,8192]{1,0:T(8,128)} fusion(bf16[2048,8192]{1,0:T(8,128)(2,1)} %param.5, bf16[512,2048]{1,0:T(8,128)(2,1)} %param.4, bf16[512,2048]{1,0:T(8,128)(2,1)} %param.3), kind=kOutput, calls=%fused_computation.7 | convolution fusion | flops 17188257792 | bytes 54525952 | tf_op jit(solution)/shard_map/dot_general | solution.py:12
  35.0 0.0 reduce-scatter.2.cloned.1.call-update
  35.1 181.4 %reduce-scatter.2.cloned.1.call-done = f32[32,8192]{1,0:T(8,128)} async-done(((f32[512,8192]{1,0:T(8,128)}), f32[32,8192]{1,0:T(8,128)}) %reduce-scatter.2.cloned.1.call-update) | async-done | bytes 1048592 | tf_op jit(solution)/shard_map/reduce_scatter | solution.py:11
  216.5 2.1 convert_element_type.15
Async XLA Ops:
  6.5 209.9 %reduce-scatter.2.cloned.1.call-start = ((), (), s32[]{:S(2)}) async-start(), calls=%async_computation.1 | async-start | bytes 17825792 | tf_op jit(solution)/shard_map/reduce_scatter | solution.py:11
Sparse Core Ops, SparseCore 0:
  35.2 181.2 reduce-scatter.1
where the time goes:
time: 226 us; the launch traced here: 225 us
  waiting for transfers between devices  181 us (80%)
  matrix products  28.5 us (13%)
  between operations  13.4 us (6%)
    reduce_scatter x1, waiting for transfers between devices, per_device(): lax.psum_scatter(jnp.dot(hidden, down_weight, preferred_element_type=jnp....  181 us
    dot_general x1, matrix products, per_device(): jnp.dot(hidden, down_weight, preferred_element_type=jnp.float32)  28.5 us
  transfers between devices with their start and end apart: 1, of which 1 were waited for; matrix products, arithmetic and copies ran while one was open for 0% of the time, Pallas kernels for 0%

commit v1 on v0

v1 whole, which is shorter than its diff:
```python
import functools

import jax
import jax.numpy as jnp
from jax import lax
from jax.experimental import pallas as pl
from jax.experimental.pallas import tpu as pltpu
from jax.sharding import PartitionSpec as P

MESH = pl.DeviceIdType.MESH
BF16 = jnp.bfloat16
F32 = jnp.float32

ZS = 4
WIDE = 4 * ZS
CHUNK = 512
SLOTS = 3


def plain_per_device(gate_pre, up_pre, down_weight):
    hidden = (jax.nn.silu(gate_pre.astype(F32)) * up_pre.astype(F32)).astype(BF16)
    summed = lax.psum_scatter(
        jnp.dot(hidden, down_weight, preferred_element_type=F32),
        "wide",
        scatter_dimension=0,
        tiled=True,
    )
    return summed.astype(BF16)


def kernel(
    steps, rows,
    gate_hbm, up_hbm, w_hbm, out_ref,
    gate, up, hidden, w_buf,
    c_send, c_recv, c_own, y_send, y_recv, y_own, z_send, z_recv, z_own,
    in_sem, w_sem, c_ssem, c_rsem, y_ssem, y_rsem, z_ssem, z_rsem,
):
    group = lax.axis_index("groups")
    me = lax.axis_index("wide")
    z, y, c = me // 4, (me // 2) % 2, me % 2

    def device(zz, yy, cc):
        return (group, zz * 4 + yy * 2 + cc)

    core_peer = device(z, y, 1 - c)
    y_peer = device(z, 1 - y, c)
    z_peers = [device(lax.rem(z + k, ZS), y, c) for k in range(1, ZS)]

    def w_copy(t):
        slot = lax.rem(t, SLOTS)
        return pltpu.make_async_copy(
            w_hbm.at[:, pl.ds(pl.multiple_of(t * CHUNK, CHUNK), CHUNK)], w_buf.at[slot], w_sem.at[slot]
        )

    def in_copies(p):
        a, b, k = p // (2 * ZS), (p // ZS) % 2, p % ZS
        owner = device(lax.rem(z + k, ZS), y if b else 1 - y, c if a else 1 - c)[1]
        src = pl.ds(pl.multiple_of(owner * rows, rows), rows)
        dst = pl.ds(p * rows, rows)
        return (
            pltpu.make_async_copy(gate_hbm.at[src], gate.at[dst], in_sem.at[0, p]),
            pltpu.make_async_copy(up_hbm.at[src], up.at[dst], in_sem.at[1, p]),
        )

    for p in range(WIDE):
        for copy in in_copies(p):
            copy.start()
    for t in range(SLOTS):
        w_copy(t).start()

    barrier = pltpu.get_barrier_semaphore()
    peers = [core_peer, y_peer] + z_peers
    for peer in peers:
        pl.semaphore_signal(barrier, inc=1, device_id=peer, device_id_type=MESH)

    for p in range(WIDE):
        for copy in in_copies(p):
            copy.wait()
        block = pl.ds(p * rows, rows)
        v = gate[block].astype(F32)
        hidden[block] = (v / (1.0 + jnp.exp(-v)) * up[block].astype(F32)).astype(BF16)

    pl.semaphore_wait(barrier, len(peers))

    def c_copy(t):
        return pltpu.make_async_remote_copy(
            c_send.at[t], c_recv.at[t], c_ssem.at[t], c_rsem.at[t], device_id=core_peer, device_id_type=MESH
        )

    def y_copy(t):
        return pltpu.make_async_remote_copy(
            y_send.at[t], y_recv.at[t], y_ssem.at[t], y_rsem.at[t], device_id=y_peer, device_id_type=MESH
        )

    def z_copy(k, t):
        return pltpu.make_async_remote_copy(
            z_send.at[k, t], z_recv.at[k, t], z_ssem.at[k, t], z_rsem.at[k, t],
            device_id=z_peers[k], device_id_type=MESH,
        )

    half, quarter = 8 * rows, 4 * rows

    def multiply(t):
        w_copy(t).wait()
        w = w_buf[lax.rem(t, SLOTS)]
        product = jnp.dot(hidden[...], w, preferred_element_type=F32)
        c_send[t] = product[:half].astype(BF16)
        c_own[t] = product[half:]
        c_copy(t).start()

        @pl.when(t + SLOTS < steps)
        def _():
            w_copy(t + SLOTS).start()

    def add_core(t):
        c_copy(t).wait_recv()
        y_send[t] = (c_own[t, :quarter] + c_recv[t, :quarter].astype(F32)).astype(BF16)
        y_copy(t).start()
        y_own[t] = c_own[t, quarter:] + c_recv[t, quarter:].astype(F32)

    def add_y(t):
        y_copy(t).wait_recv()
        for k in range(1, ZS):
            part = slice(k * rows, (k + 1) * rows)
            z_send[k - 1, t] = (y_own[t, part] + y_recv[t, part].astype(F32)).astype(BF16)
            z_copy(k - 1, t).start()
        z_own[t] = y_own[t, :rows] + y_recv[t, :rows].astype(F32)

    def add_z(t):
        total = z_own[t]
        for k in range(ZS - 1):
            z_copy(k, t).wait_recv()
            total += z_recv[k, t].astype(F32)
        out_ref[:, pl.ds(pl.multiple_of(t * CHUNK, CHUNK), CHUNK)] = total.astype(BF16)

    lags = (0, 1, 3, 6)
    stages = (multiply, add_core, add_y, add_z)

    def step(t, carry):
        for lag, stage in zip(lags, stages):
            @pl.when((t >= lag) & (t < steps + lag))
            def _(lag=lag, stage=stage):
                stage(t - lag)
        return carry

    lax.fori_loop(0, steps + lags[-1], step, 0)

    def drain(t, carry):
        c_copy(t).wait_send()
        y_copy(t).wait_send()
        for k in range(ZS - 1):
            z_copy(k, t).wait_send()
        return carry

    lax.fori_loop(0, steps, drain, 0)


def fused_per_device(gate_pre, up_pre, down_weight):
    tokens, depth = gate_pre.shape
    columns = down_weight.shape[1]
    rows, steps = tokens // WIDE, columns // CHUNK
    dma = pltpu.SemaphoreType.DMA
    return pl.pallas_call(
        functools.partial(kernel, steps, rows),
        out_shape=jax.ShapeDtypeStruct((rows, columns), BF16),
        in_specs=[pl.BlockSpec(memory_space=pl.ANY)] * 3,
        out_specs=pl.BlockSpec(memory_space=pltpu.VMEM),
        scratch_shapes=[
            pltpu.VMEM((tokens, depth), BF16),
            pltpu.VMEM((tokens, depth), BF16),
            pltpu.VMEM((tokens, depth), BF16),
            pltpu.VMEM((SLOTS, depth, CHUNK), BF16),
            pltpu.VMEM((steps, 8 * rows, CHUNK), BF16),
            pltpu.VMEM((steps, 8 * rows, CHUNK), BF16),
            pltpu.VMEM((steps, 8 * rows, CHUNK), F32),
            pltpu.VMEM((steps, 4 * rows, CHUNK), BF16),
            pltpu.VMEM((steps, 4 * rows, CHUNK), BF16),
            pltpu.VMEM((steps, 4 * rows, CHUNK), F32),
            pltpu.VMEM((ZS - 1, steps, rows, CHUNK), BF16),
            pltpu.VMEM((ZS - 1, steps, rows, CHUNK), BF16),
            pltpu.VMEM((steps, rows, CHUNK), F32),
            dma((2, WIDE)),
            dma((SLOTS,)),
            dma((steps,)),
            dma((steps,)),
            dma((steps,)),
            dma((steps,)),
            dma((ZS - 1, steps)),
            dma((ZS - 1, steps)),
        ],
        compiler_params=pltpu.CompilerParams(
            collective_id=0, has_side_effects=True, vmem_limit_bytes=60 * 2**20
        ),
        cost_estimate=pl.CostEstimate(
            flops=2 * tokens * depth * columns,
            bytes_accessed=2 * (2 * tokens * depth + depth * columns + rows * columns),
            transcendentals=tokens * depth,
        ),
    )(gate_pre, up_pre, down_weight)


def solution(mesh):
    in_specs = (P("groups", "wide"), P("groups", "wide"), P("wide", None))
    out_specs = P(("groups", "wide"), None)
    body = fused_per_device if mesh.shape["wide"] == WIDE else plain_per_device
    return jax.shard_map(body, mesh=mesh, in_specs=in_specs, out_specs=out_specs, check_vma=False)
```

time: 226 us -> 65.5 us (0.29)
  waiting for transfers between devices: 181 us -> 0 us
  Pallas kernels: 0 us -> 63.5 us
  matrix products: 28.5 us -> 0 us
  between operations: 13.4 us -> 0.01 us
    reduce_scatter x1 -> x0, waiting for transfers between devices: 181 us -> none  [per_device(): lax.psum_scatter(jnp.dot(hidden, down_weight, preferred_element_type=jnp....]
    pallas_call x0 -> x1, Pallas kernels: none -> 63.5 us  [fused_per_device(): pl.pallas_call(functools.partial(kernel, steps, rows), out_shape=jax.Shap...]
    dot_general x1 -> x0, matrix products: 28.5 us -> none  [per_device(): jnp.dot(hidden, down_weight, preferred_element_type=jnp.float32)]
  transfers between devices with their start and end apart: 1 -> 0, of which waited for: 1 -> 0; matrix products, arithmetic and copies ran while one was open for 0% -> 0% of each run, Pallas kernels for 0% -> 0%
where the time goes in v1:
time: 65.5 us; the launch traced here: 65.4 us
  Pallas kernels  63.5 us (97%)
  local copies, waits for them, and re-layouts  1.87 us (3%)
    pallas_call x1, Pallas kernels, fused_per_device(): pl.pallas_call(functools.partial(kernel, steps, rows), out_shape=jax.Shap...  63.5 us
    unnamed x1, local copies, waits for them, and re-layouts  1.87 us

profile of v1, /device:TPU:0, one launch (start us, length us, event | category | flops | bytes accessed | tf_op | source)
XLA Modules:
  0.0 65.4 jit_solution(38059590611397661)
XLA Ops:
  0.0 63.5 %shard_map.37 = bf16[32,8192]{1,0:T(8,128)(2,1)} custom-call(bf16[512,2048]{1,0:T(8,128)(2,1)} %gate_hbm.1, bf16[512,2048]{1,0:T(8,128)(2,1)} %up_hbm.1, bf16[2048,8192]{1,0:T(8,128)(2,1)} %w_hbm.1), custom_call_target="tpu_custom_call" | custom-call | flops 17179869184 | bytes 38273024 | tf_op jit(solution)/shard_map/pallas_call | solution.py:163
  63.5 1.9 %copy.5 = bf16[32,8192]{1,0:T(8,128)(2,1)} copy(bf16[32,8192]{1,0:T(8,128)(2,1)} %shard_map.37) | data formatting | bytes 1048576

commit v2 on v1

v2 whole, which is shorter than its diff:
```python
import functools

import jax
import jax.numpy as jnp
from jax import lax
from jax.experimental import pallas as pl
from jax.experimental.pallas import tpu as pltpu
from jax.sharding import PartitionSpec as P

MESH = pl.DeviceIdType.MESH
BF16 = jnp.bfloat16
F32 = jnp.float32

ZS = 4
WIDE = 4 * ZS
CHUNK = 512
SLOTS = 3
EVERY, B_CHUNKS = 5, 3
LAGS = (1, 4, 4, 7, 7, 10, 10)


def plain_per_device(gate_pre, up_pre, down_weight):
    hidden = (jax.nn.silu(gate_pre.astype(F32)) * up_pre.astype(F32)).astype(BF16)
    summed = lax.psum_scatter(
        jnp.dot(hidden, down_weight, preferred_element_type=F32),
        "wide",
        scatter_dimension=0,
        tiled=True,
    )
    return summed.astype(BF16)


def kernel(
    steps, rows,
    gate_hbm, up_hbm, w_hbm, out_ref,
    gate, up, hidden, w_buf,
    c_send, c_recv, c_own, y_send, y_recv, y_own, z_send, z_recv, z_own,
    bz_send, bz_recv, bz_own, by_send, by_recv, by_own,
    in_sem, w_sem, c_ssem, c_rsem, y_ssem, y_rsem, z_ssem, z_rsem,
):
    group = lax.axis_index("groups")
    me = lax.axis_index("wide")
    z, y, c = me // 4, (me // 2) % 2, me % 2
    zx = (z, z + 1 - 2 * (z % 2), (z + 2) % 4, 3 - z)
    edge = ((z + 1) // 2 + 1) % 2
    half, quarter = 8 * rows, 4 * rows

    def device(zz, yy, cc):
        return (group, zz * 4 + yy * 2 + cc)

    core_peer = device(z, y, 1 - c)
    y_peer = device(z, 1 - y, c)
    z_peers = [device(zx[k], y, c) for k in range(1, ZS)]

    def w_copy(t):
        slot = lax.rem(t, SLOTS)
        return pltpu.make_async_copy(
            w_hbm.at[:, pl.ds(pl.multiple_of(t * CHUNK, CHUNK), CHUNK)], w_buf.at[slot], w_sem.at[slot]
        )

    def in_copies(p):
        a, b, k = p // (2 * ZS), (p // ZS) % 2, p % ZS
        owner = device(zx[k], y if b else 1 - y, c if a else 1 - c)[1]
        src = pl.ds(pl.multiple_of(owner * rows, rows), rows)
        dst = pl.ds(p * rows, rows)
        return (
            pltpu.make_async_copy(gate_hbm.at[src], gate.at[dst], in_sem.at[0, p]),
            pltpu.make_async_copy(up_hbm.at[src], up.at[dst], in_sem.at[1, p]),
        )

    def activate(p):
        for copy in in_copies(p):
            copy.wait()
        block = pl.ds(p * rows, rows)
        v = gate[block].astype(F32)
        hidden[block] = (v / (1.0 + jnp.exp(-v)) * up[block].astype(F32)).astype(BF16)

    def c_copy(t):
        return pltpu.make_async_remote_copy(
            c_send.at[t], c_recv.at[t], c_ssem.at[t], c_rsem.at[t], device_id=core_peer, device_id_type=MESH
        )

    def y_copy(t, i, send, recv):
        return pltpu.make_async_remote_copy(
            send.at[i], recv.at[i], y_ssem.at[t], y_rsem.at[t], device_id=y_peer, device_id_type=MESH
        )

    def z_copy(k, t, i, send, recv):
        slot = 3 * (1 - edge) if k == 3 else k
        to = device(edge * zx[1] + (1 - edge) * zx[3], y, c) if k == 3 else z_peers[k - 1]
        return pltpu.make_async_remote_copy(
            send.at[k, i], recv.at[slot, i], z_ssem.at[k, t], z_rsem.at[slot, t], device_id=to, device_id_type=MESH
        )

    def z_arrival(slot, t, i, send, recv):
        return pltpu.make_async_remote_copy(
            send.at[1, i], recv.at[slot, i], z_ssem.at[1, t], z_rsem.at[slot, t],
            device_id=z_peers[0], device_id_type=MESH,
        )

    def z_start(t, i, send, recv, own, blocks):
        for k in (3, 1):
            send[k, i] = blocks(k).astype(BF16)
            z_copy(k, t, i, send, recv).start()

        @pl.when(edge == 1)
        def _():
            send[2, i] = blocks(2).astype(BF16)
            z_copy(2, t, i, send, recv).start()

        @pl.when(edge == 0)
        def _():
            own[1, i] = blocks(2)

        own[0, i] = blocks(0)

    def z_merge(t, i, send, recv, own):
        @pl.when(edge == 0)
        def _():
            z_arrival(0, t, i, send, recv).wait_recv()
            send[2, i] = (own[1, i] + recv[0, i].astype(F32)).astype(BF16)
            z_copy(2, t, i, send, recv).start()

    def z_finish(t, i, send, recv, own):
        @pl.when(edge == 0)
        def _():
            z_arrival(3, t, i, send, recv).wait_recv()
            own[0, i] = own[0, i] + recv[3, i].astype(F32)

        for k in (1, 2):
            z_arrival(k, t, i, send, recv).wait_recv()
        return own[0, i] + recv[1, i].astype(F32) + recv[2, i].astype(F32)

    a_z = (z_send, z_recv, z_own)
    b_z = (bz_send, bz_recv, bz_own)

    def store(t, total):
        out_ref[:, pl.ds(pl.multiple_of(t * CHUNK, CHUNK), CHUNK)] = total.astype(BF16)

    def multiply(t):
        w_copy(t).wait()
        product = jnp.dot(hidden[...], w_buf[lax.rem(t, SLOTS)], preferred_element_type=F32)
        c_send[t] = product[:half].astype(BF16)
        c_own[t] = product[half:]
        c_copy(t).start()

        @pl.when(t + SLOTS < steps)
        def _():
            w_copy(t + SLOTS).start()

    def core_sum(t, part):
        return c_own[t, part] + c_recv[t, part].astype(F32)

    def a_core(t):
        c_copy(t).wait_recv()
        y_send[t] = core_sum(t, slice(0, quarter)).astype(BF16)
        y_copy(t, t, y_send, y_recv).start()
        y_own[t] = core_sum(t, slice(quarter, half))

    def a_y(t):
        y_copy(t, t, y_send, y_recv).wait_recv()

        def blocks(k):
            part = slice(k * rows, (k + 1) * rows)
            return y_own[t, part] + y_recv[t, part].astype(F32)

        z_start(t, t, *a_z, blocks)

    def a_merge(t):
        z_merge(t, t, *a_z)

    def a_z_finish(t):
        store(t, z_finish(t, t, *a_z))

    def b_core(t):
        i = t // EVERY
        c_copy(t).wait_recv()

        def blocks(k):
            return jnp.concatenate(
                [core_sum(t, slice(p * rows, (p + 1) * rows)) for p in (k, ZS + k)], axis=0
            )

        z_start(t, i, *b_z, blocks)

    def b_merge(t):
        z_merge(t, t // EVERY, *b_z)

    def b_z_finish(t):
        i = t // EVERY
        total = z_finish(t, i, *b_z)
        by_send[i] = total[:rows].astype(BF16)
        y_copy(t, i, by_send, by_recv).start()
        by_own[i] = total[rows:]

    def b_y(t):
        i = t // EVERY
        y_copy(t, i, by_send, by_recv).wait_recv()
        store(t, by_own[i] + by_recv[i].astype(F32))

    def is_b(t):
        return (t % EVERY == 1) & (t // EVERY < B_CHUNKS)

    def is_a(t):
        return (t % EVERY != 1) | (t // EVERY >= B_CHUNKS)

    for p in range(WIDE // 2):
        for copy in in_copies(p):
            copy.start()
    w_copy(0).start()
    for p in range(WIDE // 2, WIDE):
        for copy in in_copies(p):
            copy.start()
    for t in range(1, SLOTS):
        w_copy(t).start()

    barrier = pltpu.get_barrier_semaphore()
    peers = [core_peer, y_peer] + z_peers
    for peer in peers:
        pl.semaphore_signal(barrier, inc=1, device_id=peer, device_id_type=MESH)

    for p in range(WIDE // 2):
        activate(p)
    w_copy(0).wait()
    c_send[0] = jnp.dot(hidden[:half], w_buf[0], preferred_element_type=F32).astype(BF16)
    pl.semaphore_wait(barrier, len(peers))
    c_copy(0).start()
    for p in range(WIDE // 2, WIDE):
        activate(p)
    c_own[0] = jnp.dot(hidden[half:], w_buf[0], preferred_element_type=F32)
    w_copy(SLOTS).start()

    schedule = (
        (LAGS[0], is_a, a_core),
        (LAGS[0], is_b, b_core),
        (LAGS[1], is_a, a_y),
        (LAGS[2], is_b, b_merge),
        (LAGS[3], is_a, a_merge),
        (LAGS[4], is_b, b_z_finish),
        (LAGS[5], is_a, a_z_finish),
        (LAGS[6], is_b, b_y),
    )

    def step(t, carry):
        @pl.when(t < steps)
        def _():
            multiply(t)

        for lag, kind, stage in schedule:
            @pl.when((t >= lag) & (t < steps + lag) & kind(t - lag))
            def _(lag=lag, stage=stage):
                stage(t - lag)
        return carry

    lax.fori_loop(1, steps + max(LAGS), step, 0)

    def drain(t, carry):
        c_copy(t).wait_send()

        @pl.when(is_a(t))
        def _():
            y_copy(t, t, y_send, y_recv).wait_send()
            for k in range(1, ZS):
                z_copy(k, t, t, z_send, z_recv).wait_send()

        @pl.when(is_b(t))
        def _():
            i = t // EVERY
            y_copy(t, i, by_send, by_recv).wait_send()
            for k in range(1, ZS):
                z_copy(k, t, i, bz_send, bz_recv).wait_send()

        return carry

    lax.fori_loop(0, steps, drain, 0)


def fused_per_device(gate_pre, up_pre, down_weight):
    tokens, depth = gate_pre.shape
    columns = down_weight.shape[1]
    rows, steps = tokens // WIDE, columns // CHUNK
    dma = pltpu.SemaphoreType.DMA
    vmem = pltpu.VMEM
    return pl.pallas_call(
        functools.partial(kernel, steps, rows),
        out_shape=jax.ShapeDtypeStruct((rows, columns), BF16),
        in_specs=[pl.BlockSpec(memory_space=pl.ANY)] * 3,
        out_specs=pl.BlockSpec(memory_space=pltpu.VMEM),
        scratch_shapes=[
            vmem((tokens, depth), BF16),
            vmem((tokens, depth), BF16),
            vmem((tokens, depth), BF16),
            vmem((SLOTS, depth, CHUNK), BF16),
            vmem((steps, 8 * rows, CHUNK), BF16),
            vmem((steps, 8 * rows, CHUNK), BF16),
            vmem((steps, 8 * rows, CHUNK), F32),
            vmem((steps, 4 * rows, CHUNK), BF16),
            vmem((steps, 4 * rows, CHUNK), BF16),
            vmem((steps, 4 * rows, CHUNK), F32),
            vmem((ZS, steps, rows, CHUNK), BF16),
            vmem((ZS, steps, rows, CHUNK), BF16),
            vmem((2, steps, rows, CHUNK), F32),
            vmem((ZS, B_CHUNKS, 2 * rows, CHUNK), BF16),
            vmem((ZS, B_CHUNKS, 2 * rows, CHUNK), BF16),
            vmem((2, B_CHUNKS, 2 * rows, CHUNK), F32),
            vmem((B_CHUNKS, rows, CHUNK), BF16),
            vmem((B_CHUNKS, rows, CHUNK), BF16),
            vmem((B_CHUNKS, rows, CHUNK), F32),
            dma((2, WIDE)),
            dma((SLOTS,)),
            dma((steps,)),
            dma((steps,)),
            dma((steps,)),
            dma((steps,)),
            dma((ZS, steps)),
            dma((ZS, steps)),
        ],
        compiler_params=pltpu.CompilerParams(
            collective_id=0, has_side_effects=True, vmem_limit_bytes=60 * 2**20
        ),
        cost_estimate=pl.CostEstimate(
            flops=2 * tokens * depth * columns,
            bytes_accessed=2 * (2 * tokens * depth + depth * columns + rows * columns),
            transcendentals=tokens * depth,
        ),
    )(gate_pre, up_pre, down_weight)


def solution(mesh):
    in_specs = (P("groups", "wide"), P("groups", "wide"), P("wide", None))
    out_specs = P(("groups", "wide"), None)
    body = fused_per_device if mesh.shape["wide"] == WIDE else plain_per_device
    return jax.shard_map(body, mesh=mesh, in_specs=in_specs, out_specs=out_specs, check_vma=False)
```

time: 65.5 us -> 61.7 us (0.942)
  Pallas kernels: 63.5 us -> 59.7 us
    pallas_call x1, Pallas kernels: 63.5 us -> 59.7 us  [fused_per_device(): pl.pallas_call(functools.partial(kernel, steps, rows), out_shape=jax.Shap...]
where the time goes in v2:
time: 61.7 us; the launch traced here: 61.6 us
  Pallas kernels  59.7 us (97%)
  local copies, waits for them, and re-layouts  1.87 us (3%)
    pallas_call x1, Pallas kernels, fused_per_device(): pl.pallas_call(functools.partial(kernel, steps, rows), out_shape=jax.Shap...  59.7 us
    unnamed x1, local copies, waits for them, and re-layouts  1.87 us

profile of v2, /device:TPU:0, one launch (start us, length us, event | category | flops | bytes accessed | tf_op | source)
XLA Modules:
  0.0 61.6 jit_solution(274655199113238675)
XLA Ops:
  0.0 59.7 %shard_map.37 = bf16[32,8192]{1,0:T(8,128)(2,1)} custom-call(bf16[512,2048]{1,0:T(8,128)(2,1)} %gate_hbm.1, bf16[512,2048]{1,0:T(8,128)(2,1)} %up_hbm.1, bf16[2048,8192]{1,0:T(8,128)(2,1)} %w_hbm.1), custom_call_target="tpu_custom_call" | custom-call | flops 17179869184 | bytes 38273024 | tf_op jit(solution)/shard_map/pallas_call | solution.py:284
  59.7 1.9 %copy.5 = bf16[32,8192]{1,0:T(8,128)(2,1)} copy(bf16[32,8192]{1,0:T(8,128)(2,1)} %shard_map.37) | data formatting | bytes 1048576
